TPU v7x, 32 devices: a whole 2x2x4 slice. The times are simulated.
32 devices in a mesh: groups: 2 (over x), rows: 16 (over z, y, core).
Axes of the slice: x: 2, y: 2, z: 4, core: 2. Of those that a mesh axis runs over, the one named last changes fastest.
Arguments:
- pair: bfloat16 [512, 256, 128], P(('groups', 'rows')), parts along dimension 0, may hold values from -6 to 6
- proj_weights: bfloat16 [6, 128, 128], replicated, may hold values from -0.5 to 0.5
- cotangent: bfloat16 [512, 256, 128], P(('groups', 'rows')), parts along dimension 0, may hold values from -8.5 to 8.5
Outputs:
- update: bfloat16 [512, 256, 128], P(('groups', 'rows')), parts along dimension 0
- pair_grad: bfloat16 [512, 256, 128], P(('groups', 'rows')), parts along dimension 0
- weight_grads: float32 [12, 128, 128], P('groups'), parts along dimension 0
There are 2 independent parts, one for each index of `groups`. A program takes and returns all parts, laid end to end along the dimension named above; an argument that names none is the same for every part. Nothing has to cross between parts.
All inputs are finite; a program needn't handle non-finite values.
Results may differ from a plain program's by a relative error of at most 0.015.
Values may be sent and summed in bfloat16 or wider, within the bound.
A program may use at most 128 MiB of HBM per device.

v0:
```python
import jax
import jax.numpy as jnp
from jax import lax
from jax.sharding import PartitionSpec as P


def layer_norm(values, along_dim):
    centred = values - jnp.mean(values, axis=along_dim, keepdims=True)
    inv_scale = lax.rsqrt(jnp.mean(centred * centred, axis=along_dim, keepdims=True) + 1e-05)
    return (centred * inv_scale, inv_scale)


def norm_backward(normed, inv_scale, upstream, along_dim):
    return (
        upstream
        - jnp.mean(upstream, axis=along_dim, keepdims=True)
        - normed * jnp.mean(upstream * normed, axis=along_dim, keepdims=True)
    ) * inv_scale


def triangle_slab(pieces):
    left_slab, right_slab = pieces
    product = lax.dot_general(
        left_slab, right_slab, (((3,), (3,)), ((0, 1), (0, 1))), preferred_element_type=jnp.float32
    )
    return (product.astype(jnp.bfloat16), left_slab, right_slab)


def edge_backward(upstream, left_slab, right_slab):
    left_part = lax.dot_general(
        upstream, right_slab, (((3,), (2,)), ((0, 1), (0, 1))), preferred_element_type=jnp.float32
    )
    right_part = lax.dot_general(
        upstream, left_slab, (((2,), (2,)), ((0, 1), (0, 1))), preferred_element_type=jnp.float32
    )
    return (left_part.astype(jnp.bfloat16), right_part.astype(jnp.bfloat16))


def body(pair, proj_weights, cotangent):
    residues = pair.shape[1]
    local_rows = pair.shape[0]
    chans = pair.shape[2]
    ranks = lax.axis_size("rows")
    slab_width = chans // ranks
    normed_in, scale_in = layer_norm(pair.astype(jnp.float32), 2)
    normed_bf = normed_in.astype(jnp.bfloat16)
    edge_pre = jnp.einsum(
        "ikd,ndc->ncik", normed_bf, proj_weights[0:4], preferred_element_type=jnp.float32
    )
    gate_pre = jnp.einsum(
        "ikd,dc->ikc", normed_bf, proj_weights[4], preferred_element_type=jnp.float32
    )
    left_sig = jax.nn.sigmoid(edge_pre[1])
    right_sig = jax.nn.sigmoid(edge_pre[3])
    left_edge = (
        (left_sig * edge_pre[0])
        .astype(jnp.bfloat16)
        .reshape(ranks, slab_width, local_rows, residues)
    )
    right_edge = (
        (right_sig * edge_pre[2])
        .astype(jnp.bfloat16)
        .reshape(ranks, slab_width, local_rows, residues)
    )
    products, left_held, right_held = triangle_slab(
        (
            lax.all_to_all(left_edge, "rows", split_axis=0, concat_axis=2, tiled=True),
            lax.all_to_all(right_edge, "rows", split_axis=0, concat_axis=2, tiled=True),
        )
    )
    regrouped = lax.all_to_all(products, "rows", split_axis=2, concat_axis=0, tiled=True).reshape(
        chans, local_rows, residues
    )
    normed_mid, scale_mid = layer_norm(regrouped.astype(jnp.float32), 0)
    mid_bf = normed_mid.astype(jnp.bfloat16)
    projected = jnp.einsum(
        "cij,cd->ijd", mid_bf, proj_weights[5], preferred_element_type=jnp.float32
    )
    gating = jax.nn.sigmoid(gate_pre)
    update = (gating * projected).astype(jnp.bfloat16)
    upstream = cotangent.astype(jnp.float32)
    gated_up = (upstream * gating).astype(jnp.bfloat16)
    gate_grad = (upstream * projected * gating * (1.0 - gating)).astype(jnp.bfloat16)
    out_weights = jnp.stack(
        [
            jnp.einsum("ikd,ikc->dc", normed_bf, gate_grad, preferred_element_type=jnp.float32),
            jnp.einsum("cij,ijd->cd", mid_bf, gated_up, preferred_element_type=jnp.float32),
        ]
    )
    mid_grad = jnp.einsum(
        "ijd,cd->cij", gated_up, proj_weights[5], preferred_element_type=jnp.float32
    )
    prod_grad = norm_backward(normed_mid, scale_mid, mid_grad, 0).astype(jnp.bfloat16)
    prod_grad = prod_grad.reshape(ranks, slab_width, local_rows, residues)
    slab_grad = lax.all_to_all(prod_grad, "rows", split_axis=0, concat_axis=2, tiled=True)
    left_part, right_part = edge_backward(slab_grad, left_held, right_held)
    left_back, right_back = (
        lax.all_to_all(left_part, "rows", split_axis=2, concat_axis=0, tiled=True),
        lax.all_to_all(right_part, "rows", split_axis=2, concat_axis=0, tiled=True),
    )
    left_full = left_back.reshape(chans, local_rows, residues).astype(jnp.float32)
    right_full = right_back.reshape(chans, local_rows, residues).astype(jnp.float32)
    edge_grad = jnp.stack(
        [
            left_full * left_sig,
            left_full * edge_pre[0] * left_sig * (1.0 - left_sig),
            right_full * right_sig,
            right_full * edge_pre[2] * right_sig * (1.0 - right_sig),
        ]
    ).astype(jnp.bfloat16)
    in_weights = jnp.einsum(
        "ikd,ncik->ndc", normed_bf, edge_grad, preferred_element_type=jnp.float32
    )
    input_grad = jnp.einsum(
        "ncik,ndc->ikd", edge_grad, proj_weights[0:4], preferred_element_type=jnp.float32
    )
    input_grad = input_grad + jnp.einsum(
        "ikc,dc->ikd", gate_grad, proj_weights[4], preferred_element_type=jnp.float32
    )
    pair_grad = norm_backward(normed_in, scale_in, input_grad, 2).astype(jnp.bfloat16)
    totals = lax.psum(
        jnp.concatenate([in_weights, out_weights], axis=0).astype(jnp.bfloat16), "rows"
    ).astype(jnp.float32)
    weight_grads = totals / residues
    return (update, pair_grad, weight_grads)


def solution(mesh):
    in_specs = (P(("groups", "rows"), None, None), P(), P(("groups", "rows"), None, None))
    out_specs = (
        P(("groups", "rows"), None, None),
        P(("groups", "rows"), None, None),
        P("groups", None, None),
    )
    return jax.shard_map(body, mesh=mesh, in_specs=in_specs, out_specs=out_specs, check_vma=False)
```

profile of v0, /device:TPU:0, one launch (start us, length us, event | category | flops | bytes accessed | tf_op | source)
XLA Modules:
  0.0 318.2 jit_solution(738744233146156121)
XLA Ops:
  7.2 1.5 copy.69
  8.9 0.3 fusion.9
  9.2 1.3 convolution_bitcast_fusion
  10.5 1.2 fusion.46
  11.7 2.0 copy-done
  13.7 1.1 copy.75
  14.8 7.4 %all-to-all-start.1 = ((bf16[16,8,16,256]{3,1,2,0:T(8,128)(2,1)}), bf16[16,8,16,256]{3,1,2,0:T(8,128)(2,1)S(1)}, u32[]{:S(2)}, u32[]{:S(2)}) async-start(bf16[16,8,16,256]{3,1,2,0:T(8,128)(2,1)} %copy.75), calls=%async_computation.1 | async-start | bytes 2097152 | tf_op jit(solution)/shard_map/all_to_all | solution.py:68
  22.2 1.1 copy.73
  23.3 21.9 %all-to-all-done.1 = bf16[16,8,16,256]{3,1,2,0:T(8,128)(2,1)S(1)} async-done(((bf16[16,8,16,256]{3,1,2,0:T(8,128)(2,1)}), bf16[16,8,16,256]{3,1,2,0:T(8,128)(2,1)S(1)}, u32[]{:S(2)}, u32[]{:S(2)}) %all-to-all-start.1) | async-done | bytes 1048608 | tf_op jit(solution)/shard_map/all_to_all | solution.py:68
  45.2 6.9 %all-to-all-start = ((bf16[16,8,16,256]{3,1,2,0:T(8,128)(2,1)}), bf16[16,8,16,256]{3,1,2,0:T(8,128)(2,1)}, u32[]{:S(2)}, u32[]{:S(2)}) async-start(bf16[16,8,16,256]{3,1,2,0:T(8,128)(2,1)} %copy.73), calls=%async_computation | async-start | bytes 2097152 | tf_op jit(solution)/shard_map/all_to_all | solution.py:67
  52.1 0.2 copy.76
  52.3 22.8 %all-to-all-done = bf16[16,8,16,256]{3,1,2,0:T(8,128)(2,1)} async-done(((bf16[16,8,16,256]{3,1,2,0:T(8,128)(2,1)}), bf16[16,8,16,256]{3,1,2,0:T(8,128)(2,1)}, u32[]{:S(2)}, u32[]{:S(2)}) %all-to-all-start) | async-done | bytes 1048608 | tf_op jit(solution)/shard_map/all_to_all | solution.py:67
  75.1 1.4 copy.74
  76.5 0.5 fusion.34
  77.0 0.6 copy.77
  77.6 31.5 %all_to_all.72 = bf16[1,8,256,256]{3,1,0,2:T(8,128)(2,1)S(1)} all-to-all(bf16[1,8,256,256]{3,1,0,2:T(8,128)(2,1)S(1)} %copy.77), channel_id=1, replica_groups=mesh['groups'=2,'rows'=16] {'rows'}, dimensions={2} | all-to-all | bytes 2097152 | tf_op jit(solution)/shard_map/all_to_all | solution.py:71
  109.1 0.3 convert_bitcast_fusion
  109.6 0.3 multiply_reduce_fusion
  110.0 0.3 multiply_convert_fusion.3
  110.4 0.6 fusion.51
  110.9 0.7 copy-done.7
  111.6 2.5 fusion.13
  114.1 1.6 bitcast_reduce_fusion
  115.8 1.6 fusion.47
  117.5 29.8 %all_to_all.73 = bf16[16,8,16,256]{3,1,2,0:T(8,128)(2,1)S(1)} all-to-all(bf16[16,8,16,256]{3,1,2,0:T(8,128)(2,1)S(1)} %copy.82), channel_id=1, replica_groups=mesh['groups'=2,'rows'=16] {'rows'}, dimensions={0} | all-to-all | bytes 2097152 | tf_op jit(solution)/shard_map/all_to_all | solution.py:95
  147.3 1.0 copy-done.4
  148.6 0.4 fusion.35
  149.0 1.6 copy.84
  150.6 5.0 %all-to-all-start.4 = ((bf16[1,8,256,256]{3,1,0,2:T(8,128)(2,1)}), bf16[1,8,256,256]{3,1,0,2:T(8,128)(2,1)}, u32[]{:S(2)}, u32[]{:S(2)}) async-start(bf16[1,8,256,256]{3,1,0,2:T(8,128)(2,1)} %copy.84), calls=%async_computation.4 | async-start | bytes 2097152 | tf_op jit(solution)/shard_map/all_to_all | solution.py:98
  155.6 2.0 fusion.36
  157.7 1.6 copy.87
  159.3 19.3 %all-to-all-done.4 = bf16[1,8,256,256]{3,1,0,2:T(8,128)(2,1)} async-done(((bf16[1,8,256,256]{3,1,0,2:T(8,128)(2,1)}), bf16[1,8,256,256]{3,1,0,2:T(8,128)(2,1)}, u32[]{:S(2)}, u32[]{:S(2)}) %all-to-all-start.4) | async-done | bytes 1048608 | tf_op jit(solution)/shard_map/all_to_all | solution.py:98
  178.6 6.9 %all-to-all-start.5 = ((bf16[1,8,256,256]{3,1,0,2:T(8,128)(2,1)}), bf16[1,8,256,256]{3,1,0,2:T(8,128)(2,1)}, u32[]{:S(2)}, u32[]{:S(2)}) async-start(bf16[1,8,256,256]{3,1,0,2:T(8,128)(2,1)} %copy.87), calls=%async_computation.5 | async-start | bytes 2097152 | tf_op jit(solution)/shard_map/all_to_all | solution.py:99
  185.5 0.3 all-reduce.2.cloned.1.call-start
  185.8 2.0 fusion.43
  187.8 2.9 fusion.42
  190.7 17.8 %all-to-all-done.5 = bf16[1,8,256,256]{3,1,0,2:T(8,128)(2,1)} async-done(((bf16[1,8,256,256]{3,1,0,2:T(8,128)(2,1)}), bf16[1,8,256,256]{3,1,0,2:T(8,128)(2,1)}, u32[]{:S(2)}, u32[]{:S(2)}) %all-to-all-start.5) | async-done | bytes 1048608 | tf_op jit(solution)/shard_map/all_to_all | solution.py:99
  208.5 5.0 %fusion.24 = (bf16[1,128,16,256]{3,1,0,2:T(8,128)(2,1)S(1)}, bf16[1,128,16,256]{3,1,0,2:T(8,128)(2,1)S(1)}, bf16[1,128,16,256]{3,1,0,2:T(8,128)(2,1)S(1)}, bf16[1,128,16,256]{3,1,0,2:T(8,128)(2,1)S(1)}) fusion(f32[4,128,16,256]{3,1,0,2:T(8,128)} %copy-done, bf16[1,8,16,16,256]{4,1,3,2,0:T(8,128)(2,1)} %bitcast.53, bf16[1,8,16,16,256]{4,1,3,2,0:T(8,128)(2,1)} %bitcast.51), kind=kLoop, calls=%fused_computation.37 | loop fusion | flops 11534336 | bytes 14680064 | tf_op jit(solution)/shard_map/convert.17
  213.5 1.3 fusion.39
  214.8 0.7 fusion.55
  215.5 0.5 copy-done.8
  216.0 0.7 fusion.77
  216.7 0.7 pad_maximum_fusion.3
  217.5 1.6 fusion.8
  219.1 2.3 copy.93
  221.3 88.2 %all-reduce.2.cloned.1.call-done = bf16[6,128,128]{1,2,0:T(8,128)(2,1)} async-done(((bf16[6,128,128]{1,2,0:T(8,128)(2,1)}), bf16[6,128,128]{1,2,0:T(8,128)(2,1)}) %all-reduce.2.cloned.1.call-update) | async-done | bytes 196624 | tf_op jit(solution)/shard_map/psum | solution.py:121
  309.5 1.0 convert_multiply_fusion.2
  310.5 0.9 copy.94
  (29 shorter events, 0.9 us)
Async XLA Ops:
  7.2 2.1 copy-start.9
  10.5 3.2 %copy-start = (f32[4,128,16,256]{3,1,0,2:T(8,128)}, f32[4,128,16,256]{3,1,0,2:T(8,128)S(1)}, u32[]{:S(2)}) copy-start(f32[4,128,16,256]{3,1,0,2:T(8,128)S(1)} %convolution_bitcast_fusion) | copy-start | bytes 25165828
  14.8 30.3 %all-to-all-start.1 = ((bf16[16,8,16,256]{3,1,2,0:T(8,128)(2,1)}), bf16[16,8,16,256]{3,1,2,0:T(8,128)(2,1)S(1)}, u32[]{:S(2)}, u32[]{:S(2)}) async-start(bf16[16,8,16,256]{3,1,2,0:T(8,128)(2,1)} %copy.75), calls=%async_computation.1 | async-start | bytes 2097152 | tf_op jit(solution)/shard_map/all_to_all | solution.py:68
  45.2 29.9 %all-to-all-start = ((bf16[16,8,16,256]{3,1,2,0:T(8,128)(2,1)}), bf16[16,8,16,256]{3,1,2,0:T(8,128)(2,1)}, u32[]{:S(2)}, u32[]{:S(2)}) async-start(bf16[16,8,16,256]{3,1,2,0:T(8,128)(2,1)} %copy.73), calls=%async_computation | async-start | bytes 2097152 | tf_op jit(solution)/shard_map/all_to_all | solution.py:67
  52.3 24.7 %copy-start.2 = (bf16[1,8,16,16,256]{4,3,2,1,0:T(8,128)(2,1)}, bf16[1,8,16,16,256]{4,3,2,1,0:T(8,128)(2,1)S(1)}, u32[]{:S(2)}) copy-start(bf16[1,8,16,16,256]{4,3,2,1,0:T(8,128)(2,1)S(1)} %copy.76) | copy-start | bytes 3145732
  76.5 1.1 copy-start.1
  110.4 1.2 copy-start.7
  114.1 1.6 copy-start.5
  117.5 31.0 %copy-start.3 = (bf16[1,8,16,16,256]{4,3,2,1,0:T(8,128)(2,1)S(1)}, bf16[1,8,16,16,256]{4,3,2,1,0:T(8,128)(2,1)}, u32[]{:S(2)}) copy-start(bf16[1,8,16,16,256]{4,3,2,1,0:T(8,128)(2,1)} %copy-done.2) | copy-start | bytes 3145732
  147.3 1.0 copy-start.4
  150.6 28.0 %all-to-all-start.4 = ((bf16[1,8,256,256]{3,1,0,2:T(8,128)(2,1)}), bf16[1,8,256,256]{3,1,0,2:T(8,128)(2,1)}, u32[]{:S(2)}, u32[]{:S(2)}) async-start(bf16[1,8,256,256]{3,1,0,2:T(8,128)(2,1)} %copy.84), calls=%async_computation.4 | async-start | bytes 2097152 | tf_op jit(solution)/shard_map/all_to_all | solution.py:98
  178.6 29.9 %all-to-all-start.5 = ((bf16[1,8,256,256]{3,1,0,2:T(8,128)(2,1)}), bf16[1,8,256,256]{3,1,0,2:T(8,128)(2,1)}, u32[]{:S(2)}, u32[]{:S(2)}) async-start(bf16[1,8,256,256]{3,1,0,2:T(8,128)(2,1)} %copy.87), calls=%async_computation.5 | async-start | bytes 2097152 | tf_op jit(solution)/shard_map/all_to_all | solution.py:99
  185.5 124.0 %all-reduce.2.cloned.1.call-start = ((), (), s32[]{:S(2)}) async-start(), calls=%async_computation.6 | async-start | bytes 393216 | tf_op jit(solution)/shard_map/psum | solution.py:121
  185.8 2.0 copy-start.6
  214.8 1.2 copy-start.8
Sparse Core Ops, SparseCore 0:
  217.6 91.8 all-reduce.1
where the time goes:
time: 319 us; the launch traced here: 318 us
  waiting for transfers between devices  170 us (53%)
  blocking collectives  61.3 us (19%)
  starting transfers between devices  26.5 us (8%)
  local copies, waits for them, and re-layouts  16.9 us (5%)
  matrix products  16.5 us (5%)
  between operations  14.4 us (5%)
  other arithmetic  12.6 us (4%)
    psum x1, waiting for transfers between devices, body(): lax.psum(jnp.concatenate([in_weights, out_weights], axis=0).astype(jnp.bf...  88.2 us
    all_to_all x1, blocking collectives, body(): lax.all_to_all(products, 'rows', split_axis=2, concat_axis=0, tiled=True)  31.5 us
    all_to_all x1, blocking collectives, body(): lax.all_to_all(prod_grad, 'rows', split_axis=0, concat_axis=2, tiled=True)  29.8 us
    all_to_all x1, waiting for transfers between devices, body(): lax.all_to_all(left_edge, 'rows', split_axis=0, concat_axis=2, tiled=True)  22.8 us
    all_to_all x1, waiting for transfers between devices, body(): lax.all_to_all(right_edge, 'rows', split_axis=0, concat_axis=2, tiled=True)  21.9 us
    all_to_all x1, waiting for transfers between devices, body(): lax.all_to_all(left_part, 'rows', split_axis=2, concat_axis=0, tiled=True)  19.3 us
    all_to_all x1, waiting for transfers between devices, body(): lax.all_to_all(right_part, 'rows', split_axis=2, concat_axis=0, tiled=True)  17.8 us
    unnamed x23, local copies, waits for them, and re-layouts  8.91 us
  transfers between devices with their start and end apart: 5, of which 5 were waited for; matrix products, arithmetic and copies ran while one was open for 4% of the time, Pallas kernels for 0%

commit v1 on v0

--- a/solution.py
+++ b/solution.py
@@ -118,8 +118,11 @@
         "ikc,dc->ikd", gate_grad, proj_weights[4], preferred_element_type=jnp.float32
     )
     pair_grad = norm_backward(normed_in, scale_in, input_grad, 2).astype(jnp.bfloat16)
-    totals = lax.psum(
-        jnp.concatenate([in_weights, out_weights], axis=0).astype(jnp.bfloat16), "rows"
+    totals = jnp.sum(
+        lax.all_gather(
+            jnp.concatenate([in_weights, out_weights], axis=0).astype(jnp.bfloat16), "rows"
+        ),
+        axis=0,
     ).astype(jnp.float32)
     weight_grads = totals / residues
     return (update, pair_grad, weight_grads)

time: 319 us -> 274 us (0.86)
  waiting for transfers between devices: 170 us -> 123 us
    psum x1 -> x0, waiting for transfers between devices: 88.2 us -> none  [body(): lax.psum(jnp.concatenate([in_weights, out_weights], axis=0).astype(jnp.bf...]
    all_gather x0 -> x1, waiting for transfers between devices: none -> 42.4 us  [body(): lax.all_gather(jnp.concatenate([in_weights, out_weights], axis=0).astype(...]
    unnamed x23 -> x36, local copies, waits for them, and re-layouts: 8.91 us -> 7.73 us
  transfers between devices with their start and end apart: 5 -> 5, of which waited for: 5 -> 5; matrix products, arithmetic and copies ran while one was open for 4% -> 6% of each run, Pallas kernels for 0% -> 0%
where the time goes in v1:
time: 274 us
  waiting for transfers between devices  123 us (45%)
  blocking collectives  61.3 us (22%)
  starting transfers between devices  26.5 us (10%)
  matrix products  19.2 us (7%)
  local copies, waits for them, and re-layouts  16.5 us (6%)
  between operations  14.5 us (5%)
  other arithmetic  12.6 us (5%)
    all_gather x1, waiting for transfers between devices, body(): lax.all_gather(jnp.concatenate([in_weights, out_weights], axis=0).astype(...  42.4 us
    all_to_all x1, blocking collectives, body(): lax.all_to_all(products, 'rows', split_axis=2, concat_axis=0, tiled=True)  31.5 us
    all_to_all x1, blocking collectives, body(): lax.all_to_all(prod_grad, 'rows', split_axis=0, concat_axis=2, tiled=True)  29.8 us
    all_to_all x1, waiting for transfers between devices, body(): lax.all_to_all(left_edge, 'rows', split_axis=0, concat_axis=2, tiled=True)  22.8 us
    all_to_all x1, waiting for transfers between devices, body(): lax.all_to_all(right_edge, 'rows', split_axis=0, concat_axis=2, tiled=True)  21.9 us
    all_to_all x1, waiting for transfers between devices, body(): lax.all_to_all(left_part, 'rows', split_axis=2, concat_axis=0, tiled=True)  19.3 us
    all_to_all x1, waiting for transfers between devices, body(): lax.all_to_all(right_part, 'rows', split_axis=2, concat_axis=0, tiled=True)  16.6 us
    unnamed x36, local copies, waits for them, and re-layouts  7.73 us
  transfers between devices with their start and end apart: 5, of which 5 were waited for; matrix products, arithmetic and copies ran while one was open for 6% of the time, Pallas kernels for 0%

profile of v1, /device:TPU:0, one launch (start us, length us, event | category | flops | bytes accessed | tf_op | source)
XLA Modules:
  0.0 273.8 jit_solution(4895416975351418070)
XLA Ops:
  7.2 1.5 copy.69
  8.9 0.3 fusion.9
  9.2 1.3 convolution_bitcast_fusion
  10.5 1.2 fusion.46
  11.7 2.0 copy-done
  13.8 1.1 copy.75
  14.9 7.4 %all-to-all-start.1 = ((bf16[16,8,16,256]{3,1,2,0:T(8,128)(2,1)}), bf16[16,8,16,256]{3,1,2,0:T(8,128)(2,1)S(1)}, u32[]{:S(2)}, u32[]{:S(2)}) async-start(bf16[16,8,16,256]{3,1,2,0:T(8,128)(2,1)} %copy.75), calls=%async_computation.1 | async-start | bytes 2097152 | tf_op jit(solution)/shard_map/all_to_all | solution.py:68
  22.2 1.1 copy.73
  23.3 21.9 %all-to-all-done.1 = bf16[16,8,16,256]{3,1,2,0:T(8,128)(2,1)S(1)} async-done(((bf16[16,8,16,256]{3,1,2,0:T(8,128)(2,1)}), bf16[16,8,16,256]{3,1,2,0:T(8,128)(2,1)S(1)}, u32[]{:S(2)}, u32[]{:S(2)}) %all-to-all-start.1) | async-done | bytes 1048608 | tf_op jit(solution)/shard_map/all_to_all | solution.py:68
  45.2 6.9 %all-to-all-start = ((bf16[16,8,16,256]{3,1,2,0:T(8,128)(2,1)}), bf16[16,8,16,256]{3,1,2,0:T(8,128)(2,1)}, u32[]{:S(2)}, u32[]{:S(2)}) async-start(bf16[16,8,16,256]{3,1,2,0:T(8,128)(2,1)} %copy.73), calls=%async_computation | async-start | bytes 2097152 | tf_op jit(solution)/shard_map/all_to_all | solution.py:67
  52.1 0.2 copy.76
  52.3 22.8 %all-to-all-done = bf16[16,8,16,256]{3,1,2,0:T(8,128)(2,1)} async-done(((bf16[16,8,16,256]{3,1,2,0:T(8,128)(2,1)}), bf16[16,8,16,256]{3,1,2,0:T(8,128)(2,1)}, u32[]{:S(2)}, u32[]{:S(2)}) %all-to-all-start) | async-done | bytes 1048608 | tf_op jit(solution)/shard_map/all_to_all | solution.py:67
  75.1 1.4 copy.74
  76.6 0.5 fusion.34
  77.0 0.6 copy.77
  77.6 31.5 %all_to_all.72 = bf16[1,8,256,256]{3,1,0,2:T(8,128)(2,1)S(1)} all-to-all(bf16[1,8,256,256]{3,1,0,2:T(8,128)(2,1)S(1)} %copy.77), channel_id=1, replica_groups=mesh['groups'=2,'rows'=16] {'rows'}, dimensions={2} | all-to-all | bytes 2097152 | tf_op jit(solution)/shard_map/all_to_all | solution.py:71
  109.2 0.3 convert_bitcast_fusion
  109.7 0.3 multiply_reduce_fusion
  110.0 0.3 multiply_convert_fusion.3
  110.4 0.6 fusion.51
  111.0 0.7 copy-done.7
  111.6 2.5 fusion.13
  114.2 1.6 bitcast_reduce_fusion
  115.8 1.6 fusion.47
  117.6 29.8 %all_to_all.73 = bf16[16,8,16,256]{3,1,2,0:T(8,128)(2,1)S(1)} all-to-all(bf16[16,8,16,256]{3,1,2,0:T(8,128)(2,1)S(1)} %copy.82), channel_id=1, replica_groups=mesh['groups'=2,'rows'=16] {'rows'}, dimensions={0} | all-to-all | bytes 2097152 | tf_op jit(solution)/shard_map/all_to_all | solution.py:95
  147.3 1.0 copy-done.4
  148.4 0.2 copy.83
  148.6 0.4 fusion.35
  149.0 1.6 copy.84
  150.6 5.0 %all-to-all-start.4 = ((bf16[1,8,256,256]{3,1,0,2:T(8,128)(2,1)}), bf16[1,8,256,256]{3,1,0,2:T(8,128)(2,1)}, u32[]{:S(2)}, u32[]{:S(2)}) async-start(bf16[1,8,256,256]{3,1,0,2:T(8,128)(2,1)} %copy.84), calls=%async_computation.4 | async-start | bytes 2097152 | tf_op jit(solution)/shard_map/all_to_all | solution.py:98
  155.7 2.0 fusion.36
  157.7 1.6 copy.87
  159.3 19.3 %all-to-all-done.4 = bf16[1,8,256,256]{3,1,0,2:T(8,128)(2,1)} async-done(((bf16[1,8,256,256]{3,1,0,2:T(8,128)(2,1)}), bf16[1,8,256,256]{3,1,0,2:T(8,128)(2,1)}, u32[]{:S(2)}, u32[]{:S(2)}) %all-to-all-start.4) | async-done | bytes 1048608 | tf_op jit(solution)/shard_map/all_to_all | solution.py:98
  178.7 6.9 %all-to-all-start.5 = ((bf16[1,8,256,256]{3,1,0,2:T(8,128)(2,1)}), bf16[1,8,256,256]{3,1,0,2:T(8,128)(2,1)}, u32[]{:S(2)}, u32[]{:S(2)}) async-start(bf16[1,8,256,256]{3,1,0,2:T(8,128)(2,1)} %copy.87), calls=%async_computation.5 | async-start | bytes 2097152 | tf_op jit(solution)/shard_map/all_to_all | solution.py:99
  185.6 0.3 all-gather.2.cloned.1.call-start
  185.9 2.6 fusion.43
  188.4 3.5 %fusion.42 = bf16[1,1,128,128]{2,3,1,0:T(8,128)(2,1)} fusion(f32[16,1,8,16,256]{4,3,0,2,1:T(8,128)S(1)} %get-tuple-element.29, f32[16,256]{1,0:T(8,128)S(1)} %add_rsqrt_fusion, f32[16,256]{1,0:T(8,128)S(1)} %broadcast_multiply_fusion.4, f32[16,256,128]{2,1,0:T(8,128)S(1)} %copy-done.6, bf16[16,256,128]{2,1,0:T(8,128)(2,1)} %param.5), kind=kOutput, calls=%fused_computation.72 | convolution fusion | flops 137379840 | bytes 5308416 | tf_op jit(solution)/shard_map/cij,ijd->cd/dot_general | solution.py:87
  192.0 16.6 %all-to-all-done.5 = bf16[1,8,256,256]{3,1,0,2:T(8,128)(2,1)} async-done(((bf16[1,8,256,256]{3,1,0,2:T(8,128)(2,1)}), bf16[1,8,256,256]{3,1,0,2:T(8,128)(2,1)}, u32[]{:S(2)}, u32[]{:S(2)}) %all-to-all-start.5) | async-done | bytes 1048608 | tf_op jit(solution)/shard_map/all_to_all | solution.py:99
  208.6 4.9 %fusion.24 = (bf16[1,128,16,256]{3,1,0,2:T(8,128)(2,1)S(1)}, bf16[1,128,16,256]{3,1,0,2:T(8,128)(2,1)S(1)}, bf16[1,128,16,256]{3,1,0,2:T(8,128)(2,1)S(1)}, bf16[1,128,16,256]{3,1,0,2:T(8,128)(2,1)S(1)}) fusion(f32[4,128,16,256]{3,1,0,2:T(8,128)} %copy-done, bf16[1,8,16,16,256]{4,1,3,2,0:T(8,128)(2,1)} %bitcast.54, bf16[1,8,16,16,256]{4,1,3,2,0:T(8,128)(2,1)} %bitcast.52), kind=kLoop, calls=%fused_computation.37 | loop fusion | flops 11534336 | bytes 14680064 | tf_op jit(solution)/shard_map/convert.19
  213.5 1.3 fusion.39
  214.9 0.8 copy.93
  215.8 2.2 fusion.55
  218.0 0.7 fusion.77
  218.8 0.7 fusion.8
  219.5 1.3 copy.95
  220.8 42.4 %all-gather.2.cloned.1.call-done = bf16[16,6,128,128]{3,2,1,0:T(8,128)(2,1)} async-done(((bf16[1,6,128,128]{3,2,1,0:T(8,128)(2,1)}), bf16[16,6,128,128]{3,2,1,0:T(8,128)(2,1)}) %all-gather.2.cloned.1.call-update) | async-done | bytes 3145744 | tf_op jit(solution)/shard_map/all_gather | solution.py:122
  263.3 2.5 reduce_sum.92
  266.0 0.9 copy.96
  (44 shorter events, 0.9 us)
Async XLA Ops:
  7.2 2.1 copy-start.11
  9.2 204.3 %copy-start.12 = (f32[16,256]{1,0:T(8,128)}, f32[16,256]{1,0:T(8,128)S(1)}, u32[]{:S(2)}) copy-start(f32[16,256]{1,0:T(8,128)S(1)} %add_rsqrt_fusion.1) | copy-start | bytes 49156
  10.5 3.2 %copy-start = (f32[4,128,16,256]{3,1,0,2:T(8,128)}, f32[4,128,16,256]{3,1,0,2:T(8,128)S(1)}, u32[]{:S(2)}) copy-start(f32[4,128,16,256]{3,1,0,2:T(8,128)S(1)} %convolution_bitcast_fusion) | copy-start | bytes 25165828
  14.9 30.3 %all-to-all-start.1 = ((bf16[16,8,16,256]{3,1,2,0:T(8,128)(2,1)}), bf16[16,8,16,256]{3,1,2,0:T(8,128)(2,1)S(1)}, u32[]{:S(2)}, u32[]{:S(2)}) async-start(bf16[16,8,16,256]{3,1,2,0:T(8,128)(2,1)} %copy.75), calls=%async_computation.1 | async-start | bytes 2097152 | tf_op jit(solution)/shard_map/all_to_all | solution.py:68
  45.2 29.9 %all-to-all-start = ((bf16[16,8,16,256]{3,1,2,0:T(8,128)(2,1)}), bf16[16,8,16,256]{3,1,2,0:T(8,128)(2,1)}, u32[]{:S(2)}, u32[]{:S(2)}) async-start(bf16[16,8,16,256]{3,1,2,0:T(8,128)(2,1)} %copy.73), calls=%async_computation | async-start | bytes 2097152 | tf_op jit(solution)/shard_map/all_to_all | solution.py:67
  52.3 24.7 %copy-start.2 = (bf16[1,8,16,16,256]{4,3,2,1,0:T(8,128)(2,1)}, bf16[1,8,16,16,256]{4,3,2,1,0:T(8,128)(2,1)S(1)}, u32[]{:S(2)}) copy-start(bf16[1,8,16,16,256]{4,3,2,1,0:T(8,128)(2,1)S(1)} %copy.76) | copy-start | bytes 3145732
  76.5 1.1 copy-start.1
  110.4 1.2 copy-start.7
  114.2 1.6 copy-start.5
  117.6 31.0 %copy-start.3 = (bf16[1,8,16,16,256]{4,3,2,1,0:T(8,128)(2,1)S(1)}, bf16[1,8,16,16,256]{4,3,2,1,0:T(8,128)(2,1)}, u32[]{:S(2)}) copy-start(bf16[1,8,16,16,256]{4,3,2,1,0:T(8,128)(2,1)} %copy-done.2) | copy-start | bytes 3145732
  147.3 1.0 copy-start.4
  150.6 28.0 %all-to-all-start.4 = ((bf16[1,8,256,256]{3,1,0,2:T(8,128)(2,1)}), bf16[1,8,256,256]{3,1,0,2:T(8,128)(2,1)}, u32[]{:S(2)}, u32[]{:S(2)}) async-start(bf16[1,8,256,256]{3,1,0,2:T(8,128)(2,1)} %copy.84), calls=%async_computation.4 | async-start | bytes 2097152 | tf_op jit(solution)/shard_map/all_to_all | solution.py:98
  178.7 29.9 %all-to-all-start.5 = ((bf16[1,8,256,256]{3,1,0,2:T(8,128)(2,1)}), bf16[1,8,256,256]{3,1,0,2:T(8,128)(2,1)}, u32[]{:S(2)}, u32[]{:S(2)}) async-start(bf16[1,8,256,256]{3,1,0,2:T(8,128)(2,1)} %copy.87), calls=%async_computation.5 | async-start | bytes 2097152 | tf_op jit(solution)/shard_map/all_to_all | solution.py:99
  185.6 77.7 %all-gather.2.cloned.1.call-start = ((), (), s32[]{:S(2)}) async-start(), calls=%async_computation.6 | async-start | bytes 3342336 | tf_op jit(solution)/shard_map/all_gather | solution.py:122
  185.9 2.6 copy-start.6
  213.5 1.3 copy-start.8
  213.5 1.3 copy-start.9
  213.5 1.3 copy-start.14
  213.5 1.3 copy-start.15
  215.8 2.3 copy-start.10
  215.8 2.3 copy-start.13
Sparse Core Ops, SparseCore 0:
  215.9 47.3 all-gather.1
